TPU v7x, 1024 devices: a whole 4x4x32 slice. The times are simulated.
1024 devices in a mesh: context: 64 (over x, z_lo), tensor: 16 (over z_hi, y, core).
Axes of the slice: x: 4, y: 4, z: 32 (z_hi: 2, z_lo: 16; z = z_hi * 16 + z_lo), core: 2. Of those that a mesh axis runs over, the one named last changes fastest.
Arguments:
- streams: bfloat16 [4096, 3, 8192], P('tensor', None, 'context'), may hold values from -6 to 6
- out_weight: bfloat16 [4096, 8192], P(None, 'tensor'), may hold values from -0.09375 to 0.09375
- cotangent: bfloat16 [8192, 8192], P('context', 'tensor'), may hold values from -6 to 6
- residues: float32 [4096, 16], P(('tensor', 'context')), may hold values from -0.0625 to 0.0625
- decay_rates: float32 [4096, 16], P(('tensor', 'context')), may hold values from 0.5 to 273
- skip_gain: float32 [4096], P(('tensor', 'context')), may hold values from 0.5 to 1.5
Outputs:
- block_out: float32 [8192, 8192], P('context', 'tensor')
- proj_grad: float32 [4096, 3, 8192], P('tensor', None, 'context')
- residue_grad: float32 [4096, 16], P(('tensor', 'context'))
- decay_grad: float32 [4096, 16], P(('tensor', 'context'))
- skip_grad: float32 [4096], P(('tensor', 'context'))
All inputs are finite; a program needn't handle non-finite values.
Results may differ from a plain program's by a relative error of at most 0.0029.
Values may be sent and summed in bfloat16 or wider, within the bound.
A program may use at most 32 MiB of HBM per device.

v0:
```python
import math

import jax
import jax.numpy as jnp
from jax import lax
from jax.sharding import PartitionSpec as P

HIGHEST_PRECISION = lax.Precision.HIGHEST


def tables(rows_count, cols_count, modulus):
    row_index = lax.broadcasted_iota(jnp.int32, (rows_count, cols_count), 0)
    col_index = lax.broadcasted_iota(jnp.int32, (rows_count, cols_count), 1)
    phases = (row_index * col_index % modulus).astype(jnp.float32) * (2.0 * math.pi / modulus)
    return (jnp.cos(phases), jnp.sin(phases))


def forward_spectrum(signal, size_a, size_b):
    batch = signal.shape[0]
    padding = jnp.zeros((batch, size_a * size_b - signal.shape[1]), jnp.float32)
    shaped = jnp.concatenate([signal, padding], axis=1).reshape(batch, size_a, size_b)
    cos_a, sin_a = tables(size_a, size_a, size_a)
    section_re = jnp.einsum("kn,mnb->mkb", cos_a, shaped, precision=HIGHEST_PRECISION)
    section_im = -jnp.einsum("kn,mnb->mkb", sin_a, shaped, precision=HIGHEST_PRECISION)
    cos_t, sin_t = tables(size_a, size_b, size_a * size_b)
    twist_re = section_re * cos_t + section_im * sin_t
    twist_im = section_im * cos_t - section_re * sin_t
    cos_b, sin_b = tables(size_b, size_b, size_b)
    out_re = jnp.einsum("mkn,nb->mkb", twist_re, cos_b, precision=HIGHEST_PRECISION) + jnp.einsum(
        "mkn,nb->mkb", twist_im, sin_b, precision=HIGHEST_PRECISION
    )
    out_im = jnp.einsum("mkn,nb->mkb", twist_im, cos_b, precision=HIGHEST_PRECISION) - jnp.einsum(
        "mkn,nb->mkb", twist_re, sin_b, precision=HIGHEST_PRECISION
    )
    return (out_re, out_im)


def inverse_real(spec_re, spec_im, size_a, size_b, length):
    cos_b, sin_b = tables(size_b, size_b, size_b)
    section_re = (
        jnp.einsum("mkn,nb->mkb", spec_re, cos_b, precision=HIGHEST_PRECISION)
        - jnp.einsum("mkn,nb->mkb", spec_im, sin_b, precision=HIGHEST_PRECISION)
    ) / size_b
    section_im = (
        jnp.einsum("mkn,nb->mkb", spec_im, cos_b, precision=HIGHEST_PRECISION)
        + jnp.einsum("mkn,nb->mkb", spec_re, sin_b, precision=HIGHEST_PRECISION)
    ) / size_b
    cos_t, sin_t = tables(size_a, size_b, size_a * size_b)
    twist_re = section_re * cos_t - section_im * sin_t
    twist_im = section_im * cos_t + section_re * sin_t
    cos_a, sin_a = tables(size_a, size_a, size_a)
    signal = (
        jnp.einsum("kn,mkb->mnb", cos_a, twist_re, precision=HIGHEST_PRECISION)
        - jnp.einsum("kn,mkb->mnb", sin_a, twist_im, precision=HIGHEST_PRECISION)
    ) / size_a
    return signal.reshape(signal.shape[0], size_a * size_b)[:, :length]


def local(streams, out_weight, cotangent, residues, decay_rates, skip_gain):
    local_channels = streams.shape[0]
    projected = streams.astype(jnp.float32)
    query_rows = projected[:, 0]
    key_rows = projected[:, 1]
    value_rows = projected[:, 2]
    weight_rows = out_weight
    summed = lax.psum(
        lax.dot_general(
            weight_rows, cotangent, (((1,), (1,)), ((), ())), preferred_element_type=jnp.float32
        ),
        "tensor",
    )
    grad_gated = lax.dynamic_slice_in_dim(
        summed, lax.axis_index("tensor") * local_channels, local_channels, 0
    )
    product_rows = key_rows * value_rows
    grad_conv = grad_gated * query_rows
    moved_mix, moved_grad = (
        lax.all_to_all(product_rows, "context", split_axis=0, concat_axis=1, tiled=True),
        lax.all_to_all(grad_conv, "context", split_axis=0, concat_axis=1, tiled=True),
    )
    length = moved_mix.shape[1]
    batch = moved_mix.shape[0]
    twice_len = 2 * length
    size_a = 1 << (twice_len.bit_length() - 1) // 2
    size_b = twice_len // size_a
    positions = jnp.arange(length, dtype=jnp.float32) / length
    decays = jnp.exp(-decay_rates[:, :, None] * positions[None, None, :])
    filter_rows = jnp.einsum("mr,mrt->mt", residues, decays, precision=HIGHEST_PRECISION)
    spec_re, spec_im = forward_spectrum(
        jnp.concatenate([moved_mix, filter_rows, moved_grad], axis=0), size_a, size_b
    )
    mix_re, filter_re, grad_re = (spec_re[:batch], spec_re[batch : 2 * batch], spec_re[2 * batch :])
    mix_im, filter_im, grad_im = (spec_im[:batch], spec_im[batch : 2 * batch], spec_im[2 * batch :])
    joint_re = jnp.concatenate(
        [
            mix_re * filter_re - mix_im * filter_im,
            filter_re * grad_re + filter_im * grad_im,
            mix_re * grad_re + mix_im * grad_im,
        ],
        axis=0,
    )
    joint_im = jnp.concatenate(
        [
            mix_re * filter_im + mix_im * filter_re,
            filter_re * grad_im - filter_im * grad_re,
            mix_re * grad_im - mix_im * grad_re,
        ],
        axis=0,
    )
    signals = inverse_real(joint_re, joint_im, size_a, size_b, length)
    conv_rows = signals[:batch] + skip_gain[:, None] * moved_mix
    back_rows = signals[batch : 2 * batch] + skip_gain[:, None] * moved_grad
    filter_grad = signals[2 * batch :]
    residue_grad = jnp.einsum("mrt,mt->mr", decays, filter_grad, precision=HIGHEST_PRECISION)
    decay_grad = -residues * jnp.einsum(
        "mrt,mt->mr", decays, filter_grad * positions[None, :], precision=HIGHEST_PRECISION
    )
    skip_grad = jnp.sum(moved_grad * moved_mix, axis=1)
    conv_local, back_local = (
        lax.all_to_all(conv_rows, "context", split_axis=1, concat_axis=0, tiled=True),
        lax.all_to_all(back_rows, "context", split_axis=1, concat_axis=0, tiled=True),
    )
    gated = (query_rows * conv_local).astype(jnp.bfloat16)
    weight_rows = out_weight
    block_out = lax.dot_general(
        lax.all_gather(gated, "tensor", axis=0, tiled=True),
        weight_rows,
        (((0,), (0,)), ((), ())),
        preferred_element_type=jnp.float32,
    )
    proj_grad = jnp.stack(
        [grad_gated * conv_local, back_local * value_rows, back_local * key_rows], axis=1
    )
    return (block_out, proj_grad, residue_grad, decay_grad, skip_grad)


def solution(mesh):
    return jax.shard_map(
        local,
        mesh=mesh,
        in_specs=(
            P("tensor", None, "context"),
            P(None, "tensor"),
            P("context", "tensor"),
            P(("tensor", "context"), None),
            P(("tensor", "context"), None),
            P(("tensor", "context")),
        ),
        out_specs=(
            P("context", "tensor"),
            P("tensor", None, "context"),
            P(("tensor", "context"), None),
            P(("tensor", "context"), None),
            P(("tensor", "context")),
        ),
        check_vma=False,
    )
```

profile of v0, /device:TPU:1, one launch (start us, length us, event | category | flops | bytes accessed | tf_op | source)
XLA Modules:
  0.0 690.1 jit_solution(5278843464968165862)
XLA Ops:
  7.2 0.0 copy-start
  7.2 0.0 all-reduce.3.cloned.1.call-start
  7.2 0.8 copy-done
  8.1 4.8 fusion.126
  12.8 0.0 copy-start.1
  12.8 0.0 copy-start.3
  12.8 0.0 copy-start.2
  12.8 0.0 all-reduce.3.cloned.1.call-update
  12.9 0.9 copy-done.1
  13.8 0.7 slice_multiply_fusion
  14.5 29.8 %all-to-all-start = ((f32[64,4,128]{2,1,0:T(4,128)}), f32[64,4,128]{2,1,0:T(4,128)S(1)}, u32[]{:S(2)}, u32[]{:S(2)}) async-start(f32[64,4,128]{2,1,0:T(4,128)} %bitcast.1), calls=%async_computation | async-start | bytes 262144 | tf_op jit(solution)/shard_map/all_to_all | solution.py:78
  44.3 418.9 %all-reduce.3.cloned.1.call-done = f32[4096,128]{1,0:T(8,128)} async-done(((f32[4096,128]{1,0:T(8,128)}), f32[4096,128]{1,0:T(8,128)}) %all-reduce.3.cloned.1.call-update) | async-done | bytes 2097168 | tf_op jit(solution)/shard_map/psum | solution.py:66
  463.2 1.6 fusion.34
  464.8 0.0 all-to-all-done
  464.8 20.7 %all-to-all-start.1 = ((f32[64,4,128]{2,1,0:T(4,128)}), f32[64,4,128]{2,1,0:T(4,128)S(1)}, u32[]{:S(2)}, u32[]{:S(2)}) async-start(f32[64,4,128]{2,1,0:T(4,128)} %bitcast.7), calls=%async_computation.1 | async-start | bytes 262144 | tf_op jit(solution)/shard_map/all_to_all | solution.py:79
  485.4 0.2 all-gather.2.cloned.1.call-start
  485.7 0.0 copy-done.3
  485.7 0.0 copy-done.2
  485.7 1.5 fusion.2
  487.2 0.1 copy.53
  487.3 0.3 fusion.59
  487.6 0.1 copy.20
  487.7 0.3 fusion.58
  488.0 0.1 copy.22
  488.1 0.3 broadcast_multiply_fusion
  488.3 19.3 %all-to-all-done.1 = f32[64,4,128]{2,1,0:T(4,128)S(1)} async-done(((f32[64,4,128]{2,1,0:T(4,128)}), f32[64,4,128]{2,1,0:T(4,128)S(1)}, u32[]{:S(2)}, u32[]{:S(2)}) %all-to-all-start.1) | async-done | bytes 131104 | tf_op jit(solution)/shard_map/all_to_all | solution.py:79
  507.7 0.1 select_maximum_fusion
  507.8 0.2 copy.46
  508.0 1.5 convolution_bitcast_fusion
  509.5 1.5 fusion.3
  511.1 1.6 fusion.27
  512.7 1.6 fusion.28
  514.3 1.6 convolution_add_fusion.1
  515.9 1.8 convolution_subtract_fusion.2
  517.7 0.1 multiply_add_fusion.3
  517.8 0.1 multiply_subtract_fusion.3
  517.9 1.0 fusion.22
  519.0 1.0 fusion.21
  520.0 1.0 convolution_subtract_fusion.1
  521.0 1.0 convolution_add_fusion
  522.0 1.6 fusion.15
  523.6 1.6 fusion.5
  525.3 0.3 copy.29
  525.5 0.0 copy-start.4
  525.5 0.1 pad.16
  525.6 0.6 copy.47
  526.2 0.0 copy-done.4
  526.3 0.8 multiply_bitcast_fusion
  527.0 29.5 %all_to_all.73 = f32[4,64,128]{2,0,1:T(4,128)S(1)} all-to-all(f32[4,64,128]{2,0,1:T(4,128)S(1)} %get-tuple-element.15), channel_id=1, replica_groups=mesh['context'=64,'tensor'=16] {'context'}, dimensions={1} | all-to-all | bytes 262144 | tf_op jit(solution)/shard_map/all_to_all | solution.py:120
  556.5 1.6 multiply_bitcast_fusion.1
  558.1 0.0 all-gather.2.cloned.1.call-update
  558.1 7.4 %all-to-all-start.3 = ((f32[4,64,128]{2,0,1:T(4,128)}), f32[4,64,128]{2,0,1:T(4,128)S(1)}, u32[]{:S(2)}, u32[]{:S(2)}) async-start(f32[4,64,128]{2,0,1:T(4,128)} %get-tuple-element.16), calls=%async_computation.3 | async-start | bytes 262144 | tf_op jit(solution)/shard_map/all_to_all | solution.py:121
  565.6 0.7 fusion.31
  566.3 2.9 fusion
  569.2 0.6 negate_multiply_fusion
  569.8 3.7 fusion.1
  573.5 14.1 %all-to-all-done.3 = f32[4,64,128]{2,0,1:T(4,128)S(1)} async-done(((f32[4,64,128]{2,0,1:T(4,128)}), f32[4,64,128]{2,0,1:T(4,128)S(1)}, u32[]{:S(2)}, u32[]{:S(2)}) %all-to-all-start.3) | async-done | bytes 131104 | tf_op jit(solution)/shard_map/all_to_all | solution.py:121
  587.6 0.8 pad_maximum_fusion.6
  588.3 91.0 %all-gather.2.cloned.1.call-done = bf16[4096,128]{1,0:T(8,128)(2,1)} async-done(((bf16[256,128]{1,0:T(8,128)(2,1)}), bf16[4096,128]{1,0:T(8,128)(2,1)}) %all-gather.2.cloned.1.call-update) | async-done | bytes 1048592 | tf_op jit(solution)/shard_map/all_gather | solution.py:126
  679.3 4.0 fusion.127
  (4 shorter events, 0.1 us)
Async XLA Ops:
  7.2 0.9 copy-start
  7.2 456.0 %all-reduce.3.cloned.1.call-start = ((), (), s32[]{:S(2)}) async-start(), calls=%async_computation.4 | async-start | bytes 4194304 | tf_op jit(solution)/shard_map/psum | solution.py:66
  12.8 0.9 copy-start.1
  12.8 472.8 %copy-start.3 = (f32[4,16]{1,0:T(4,128)S(1)}, f32[4,16]{1,0:T(4,128)}, u32[]{:S(2)}) copy-start(f32[4,16]{1,0:T(4,128)} %param.10) | copy-start | bytes 772
  12.8 472.9 %copy-start.2 = (f32[4,16]{1,0:T(4,128)S(1)}, f32[4,16]{1,0:T(4,128)}, u32[]{:S(2)}) copy-start(f32[4,16]{1,0:T(4,128)} %param.9) | copy-start | bytes 772
  14.5 450.3 %all-to-all-start = ((f32[64,4,128]{2,1,0:T(4,128)}), f32[64,4,128]{2,1,0:T(4,128)S(1)}, u32[]{:S(2)}, u32[]{:S(2)}) async-start(f32[64,4,128]{2,1,0:T(4,128)} %bitcast.1), calls=%async_computation | async-start | bytes 262144 | tf_op jit(solution)/shard_map/all_to_all | solution.py:78
  464.8 42.9 %all-to-all-start.1 = ((f32[64,4,128]{2,1,0:T(4,128)}), f32[64,4,128]{2,1,0:T(4,128)S(1)}, u32[]{:S(2)}, u32[]{:S(2)}) async-start(f32[64,4,128]{2,1,0:T(4,128)} %bitcast.7), calls=%async_computation.1 | async-start | bytes 262144 | tf_op jit(solution)/shard_map/all_to_all | solution.py:79
  485.4 193.9 %all-gather.2.cloned.1.call-start = ((), (), s32[]{:S(2)}) async-start(), calls=%async_computation.5 | async-start | bytes 1114112 | tf_op jit(solution)/shard_map/all_gather | solution.py:126
  525.5 0.7 copy-start.4
  558.1 29.4 %all-to-all-start.3 = ((f32[4,64,128]{2,0,1:T(4,128)}), f32[4,64,128]{2,0,1:T(4,128)S(1)}, u32[]{:S(2)}, u32[]{:S(2)}) async-start(f32[4,64,128]{2,0,1:T(4,128)} %get-tuple-element.16), calls=%async_computation.3 | async-start | bytes 262144 | tf_op jit(solution)/shard_map/all_to_all | solution.py:121
Sparse Core Ops, SparseCore 0:
  13.0 450.1 all-reduce.2
  558.2 121.0 all-gather.1
where the time goes:
time: 691 us; the launch traced here: 690 us
  waiting for transfers between devices  543 us (79%)
  starting transfers between devices  58.2 us (8%)
  matrix products  33.8 us (5%)
  blocking collectives  29.5 us (4%)
  between operations  14.3 us (2%)
  other arithmetic  7.86 us (1%)
    psum x1, waiting for transfers between devices, local(): lax.psum(lax.dot_general(weight_rows, cotangent, (((1,), (1,)), ((), ()))...  419 us
    all_gather x1, waiting for transfers between devices, local(): lax.all_gather(gated, 'tensor', axis=0, tiled=True)  91 us
    all_to_all x1, starting transfers between devices, local(): lax.all_to_all(product_rows, 'context', split_axis=0, concat_axis=1, tile...  29.8 us
    all_to_all x1, blocking collectives, local(): lax.all_to_all(conv_rows, 'context', split_axis=1, concat_axis=0, tiled=T...  29.5 us
    all_to_all x1, starting transfers between devices, local(): lax.all_to_all(grad_conv, 'context', split_axis=0, concat_axis=1, tiled=T...  20.7 us
    all_to_all x1, waiting for transfers between devices, local(): lax.all_to_all(grad_conv, 'context', split_axis=0, concat_axis=1, tiled=T...  19.3 us
    all_to_all x1, waiting for transfers between devices, local(): lax.all_to_all(back_rows, 'context', split_axis=1, concat_axis=0, tiled=T...  14.1 us
  transfers between devices with their start and end apart: 5, of which 4 were waited for; matrix products, arithmetic and copies ran while one was open for 2% of the time, Pallas kernels for 0%

commit v1 on v0

v1 whole, which is shorter than its diff:
```python
import functools

import jax
import jax.numpy as jnp
from jax import lax
from jax.experimental import pallas as pl
from jax.experimental.pallas import tpu as pltpu
from jax.sharding import PartitionSpec as P

MESH = pl.DeviceIdType.MESH
F32, BF16 = jnp.float32, jnp.bfloat16
HIGHEST = lax.Precision.HIGHEST
SEQ = 8192.0
CTX = 64
CHUNK = 128
SUB, STEPS = 8, 16
LANES = 128
GROUPS = 2
OWNERS = 4
OROWS = 8
GROWS = 24


def owner_of(o):
    return o * 16 + 7 + o % 2


def remote(src, dst, send, recv, device):
    return pltpu.make_async_remote_copy(
        src_ref=src, dst_ref=dst, send_sem=send, recv_sem=recv, device_id=device, device_id_type=MESH
    )


def dot(a, b):
    return jnp.dot(a, b, preferred_element_type=F32)


def dot_nt(a, b):
    return lax.dot_general(a, b, (((1,), (1,)), ((), ())), preferred_element_type=F32)


def kernel(
    res_hbm, dec_hbm, skip_hbm, qkv_hbm, cot_hbm, w_hbm,
    out_ref, proj_ref, res_ref, dec_ref, skip_ref,
    res_in, dec_in, skip_in, qkv_in, cot_in, w_ref,
    packed, g_all, g_two, psend, pown, prx, ysend, yrx, zsend, zrx,
    etx, erx, stx, sin, btx, brx, otx, bin_, gtx, grx, gsum, frx, ktx, krx, ksum, kfin,
    a_t, r_t, f_t, v_t, a16_t, ek_t, bk_t, a128_t, skip_t,
    qs, ks, vs, mix, grad, gconv, conv, back, turn, gall,
    sem_s, sem_r, ag_s, ag_r, sem_l,
):
    me = lax.axis_index("context")
    tensor = lax.axis_index("tensor")
    zh, y, c = tensor // 8, (tensor // 2) % 4, tensor % 2

    def at(zh_, y_, c_):
        return zh_ * 8 + y_ * 2 + c_

    def tdev(zh_, y_, c_):
        return (me, at(zh_, y_, c_))

    def cdev(j):
        return (j, tensor)

    ys = [lax.rem(y + d, 4) for d in range(4)]
    barrier = pltpu.get_barrier_semaphore()

    @pl.loop(1, CTX)
    def _(i):
        pl.semaphore_signal(barrier, inc=1, device_id=cdev(lax.rem(me + i, CTX)), device_id_type=MESH)

    for device in [tdev(1 - zh, y, c), tdev(zh, y, 1 - c)] + [tdev(zh, ys[d], c) for d in (1, 2, 3)]:
        pl.semaphore_signal(barrier, inc=1, device_id=device, device_id_type=MESH)

    loads = [
        pltpu.make_async_copy(src, dst, sem_l.at[k])
        for k, (src, dst) in enumerate(
            [(res_hbm, res_in), (dec_hbm, dec_in), (skip_hbm, skip_in), (cot_hbm, cot_in), (w_hbm, w_ref), (qkv_hbm, qkv_in)]
        )
    ]
    for load in loads:
        load.start()
    for load in loads[:3]:
        load.wait()
    lane = lax.broadcasted_iota(jnp.int32, (16, LANES), 1) % 32
    mode = lax.broadcasted_iota(jnp.int32, (16, LANES), 0)
    spread = jnp.dot(
        res_in[...], jnp.where(lane == mode, 1.0, 0.0).astype(F32), precision=HIGHEST, preferred_element_type=F32
    ) + jnp.dot(
        dec_in[...], jnp.where(lane == mode + 16, 1.0, 0.0).astype(F32), precision=HIGHEST, preferred_element_type=F32
    )
    keep = lax.broadcasted_iota(jnp.int32, (4, LANES), 1) // 32 == lax.broadcasted_iota(jnp.int32, (4, LANES), 0)
    packed[0:1, :] = jnp.sum(jnp.where(keep, spread, 0.0), axis=0, keepdims=True)
    apart = lax.broadcasted_iota(jnp.int32, (4, LANES), 1) == 32 * lax.broadcasted_iota(jnp.int32, (4, LANES), 0)
    packed[1:2, :] = jnp.dot(
        skip_in[...], jnp.where(apart, 1.0, 0.0).astype(F32), precision=HIGHEST, preferred_element_type=F32
    )
    g_all[me] = packed[...]

    def weight(block):
        return w_ref[pl.ds(pl.multiple_of(block * 256, 256), 256), :]

    for load in loads[3:5]:
        load.wait()
    cot = cot_in[...]
    for h in range(2):
        zt = 1 - zh if h == 0 else zh
        for d in range(4):
            psend[h, pl.ds(d * CHUNK, CHUNK), :] = dot_nt(cot, weight(at(zt, ys[d], 1 - c)))
            pown[h, pl.ds(d * CHUNK, CHUNK), :] = dot_nt(cot, weight(at(zt, ys[d], c)))

    def tile(ref, step, g):
        return ref[g, pl.ds(step * 8, 8), :]

    def by_step(src, dst):
        for g in range(GROUPS):
            for step in range(STEPS):
                dst[g, pl.ds(step * 8, 8), :] = src[g, pl.ds(step, 8, stride=STEPS), :]

    loads[5].wait()
    for j, dst in enumerate((qs, ks, vs)):
        for g in range(GROUPS):
            turn[g] = qkv_in[j, pl.ds(g * LANES, LANES), :].astype(F32).T
        by_step(turn, dst)
    mix[...] = ks[...] * vs[...]
    pl.semaphore_wait(barrier, CTX - 1 + 5)

    core = [
        remote(psend.at[h], prx.at[h], sem_s.at[h], sem_r.at[h], tdev(zh, y, 1 - c)) for h in range(2)
    ]
    core[0].start()

    @pl.loop(1, CTX)
    def _(i):
        remote(packed, g_all.at[me], sem_s.at[2], sem_r.at[2], cdev(lax.rem(me + i, CTX))).start()

    core[1].start()
    sums = []
    for h in range(2):
        core[h].wait_recv()
        copies = []
        for d in (1, 2, 3):
            rows = pl.ds(d * CHUNK, CHUNK)
            ysend[h, d - 1] = pown[h, rows, :] + prx[h, rows, :]
            k = 4 + h * 3 + d - 1
            copy = remote(
                ysend.at[h, d - 1], yrx.at[h, d - 1], sem_s.at[k], sem_r.at[k], tdev(zh, ys[d], c)
            )
            copy.start()
            copies.append(copy)
        sums.append(copies)

    def summed(h):
        rows = pl.ds(0, CHUNK)
        total = pown[h, rows, :] + prx[h, rows, :]
        for d in range(3):
            sums[h][d].wait_recv()
            total = total + yrx[h, d]
        return total

    zsend[...] = summed(0)
    zcopy = remote(zsend, zrx, sem_s.at[10], sem_r.at[10], tdev(1 - zh, y, c))
    zcopy.start()
    pown[1, pl.ds(0, CHUNK), :] = summed(1)

    remote(g_all.at[pl.ds(0, CTX - 1)], g_all.at[pl.ds(0, CTX - 1)], sem_s.at[2], sem_r.at[2], cdev(me)).wait()
    for j in range(CTX):
        g_two[pl.ds(j, 1), :] = g_all[j, 0:1, :]
        g_two[pl.ds(CTX + j, 1), :] = g_all[j, 1:2, :]
    turned = g_two[...].T
    source = lax.broadcasted_iota(jnp.int32, (LANES, 512), 0)
    target = lax.broadcasted_iota(jnp.int32, (LANES, 512), 1)
    params = jnp.zeros((32, 512), F32)
    for i in range(4):
        place = jnp.where(target == source * 4 + i, 1.0, 0.0).astype(F32)
        params += jnp.dot(turned[i * 32 : i * 32 + 32, :], place, precision=HIGHEST, preferred_element_type=F32)
    sub = lax.broadcasted_iota(jnp.int32, (SUB, LANES), 0)
    subf = sub.astype(F32)
    for g in range(GROUPS):
        lanes = slice(g * LANES, (g + 1) * LANES)
        skip_t[pl.ds(g * 8, 8), :] = jnp.broadcast_to(params[0:1, 256 + g * LANES : 256 + (g + 1) * LANES], (8, LANES))
        for r in range(16):
            idx = r * 2 + g
            rows = pl.ds(idx * 8, 8)
            rate = jnp.broadcast_to(params[16 + r : 17 + r, lanes], (8, LANES)) * (-1.0 / SEQ)
            r_t[rows, :] = jnp.broadcast_to(params[r : r + 1, lanes], (8, LANES))
            a_t[rows, :] = jnp.exp(rate)
            a16_t[rows, :] = jnp.exp(rate * 16.0)
            f_t[rows, :] = jnp.exp(rate * (16.0 * subf))
            v_t[rows, :] = jnp.exp(rate * (16.0 * (7.0 - subf)))
            a128_t[pl.ds(idx, 1), :] = jnp.exp(rate[0:1, :] * 128.0)

    def rows_of(i, u, g):
        return pl.ds(pl.multiple_of(i * 64 + (u * 2 + g) * 8, 8), 8)

    def eight(i):
        return pl.ds(pl.multiple_of(i * 8, 8), 8)

    def collapse(x):
        return jnp.sum(x, axis=0, keepdims=True)

    mine = me // 16
    is_owner = lax.rem(me, 16) == 7 + lax.rem(mine, 2)

    def send_to_owner(o, src, dst, k):
        @pl.when(me != owner_of(o))
        def _():
            remote(src, dst, sem_s.at[k], sem_r.at[k], cdev(owner_of(o))).start()

        @pl.when(me == owner_of(o))
        def _():
            pltpu.make_async_copy(src, dst, sem_r.at[k]).start()

    def send_to_owners(tx, rx, rows, k):
        for o in range(OWNERS):
            send_to_owner(o, tx.at[pl.ds(o * rows, rows)], rx.at[pl.ds(pl.multiple_of(me * rows, 8), rows)], k)

    def wait_sent(ref, k):
        remote(ref, ref, sem_s.at[k], sem_r.at[k], cdev(me)).wait_send()

    def sent_to_owners(tx, rows, k):
        @pl.when(is_owner)
        def _():
            wait_sent(tx.at[pl.ds(0, 3 * rows)], k)

        @pl.when(jnp.logical_not(is_owner))
        def _():
            wait_sent(tx, k)

    def from_owner(source_of, dst, k):
        @pl.loop(0, CTX)
        def _(j):
            src = source_of(j)

            @pl.when(j != me)
            def _():
                remote(src, dst, sem_s.at[k], sem_r.at[k], cdev(j)).start()

            @pl.when(j == me)
            def _():
                pltpu.make_async_copy(src, dst, sem_r.at[k]).start()

    def wait_all(ref, k):
        remote(ref, ref, sem_s.at[k], sem_r.at[k], cdev(me)).wait_recv()

    @pl.loop(0, 4)
    def _(i):
        ends = []
        for u in range(4):
            for g in range(GROUPS):
                rows = rows_of(i, u, g)
                a = a_t[rows, :]
                s = tile(mix, 0, g)
                for step in range(1, STEPS):
                    s = a * s + tile(mix, step, g)
                ek_t[rows, :] = s
                ends.append(collapse(v_t[rows, :] * s))
        etx[eight(i), :] = jnp.concatenate(ends, axis=0)

    send_to_owners(etx, erx, OROWS, 11)

    @pl.when(is_owner)
    def _():
        decay = a128_t[eight(mine), :]
        wait_all(erx, 11)

        def forward(j, s):
            stx[eight(j), :] = s
            return decay * s + erx[eight(j), :]

        lax.fori_loop(0, CTX, forward, jnp.zeros((8, LANES), F32))
        from_owner(lambda j: stx.at[eight(j)], sin.at[eight(mine)], 13)

    zcopy.wait_recv()
    for g in range(GROUPS):
        lanes = pl.ds(g * LANES, LANES)
        turn[g] = pown[1, pl.ds(0, CHUNK), lanes] + zrx[:, lanes]
    by_step(turn, grad)
    gconv[...] = grad[...] * qs[...]

    @pl.loop(0, 4)
    def _(i):
        ends = []
        for u in range(4):
            for g in range(GROUPS):
                rows = rows_of(i, u, g)
                a = a_t[rows, :]
                b = tile(gconv, STEPS - 1, g)
                for step in range(STEPS - 2, -1, -1):
                    b = a * b + tile(gconv, step, g)
                bk_t[rows, :] = b
                ends.append(collapse(f_t[rows, :] * b))
        btx[eight(i), :] = jnp.concatenate(ends, axis=0)

    send_to_owners(btx, brx, OROWS, 12)
    for g in range(GROUPS):
        ktx[pl.ds(g, 1), :] = collapse(collapse(gconv[g] * mix[g]))
    send_to_owner(0, ktx, krx.at[me], 17)

    def starts(rows, ends_t, toward):
        x = ends_t[rows, :]
        a = a16_t[rows, :]
        for reach in (0, 1, 2, 4):
            shift = max(reach, 1)
            inside = sub >= shift if toward > 0 else sub < SUB - shift
            moved = jnp.where(inside, pltpu.roll(x, shift if toward > 0 else SUB - shift, 0), 0.0)
            if reach == 0:
                x = moved
            else:
                x = x + a * moved
                a = a * a
        return x

    for g in range(GROUPS):
        for step in range(STEPS):
            conv[g, pl.ds(step * 8, 8), :] = skip_t[pl.ds(g * 8, 8), :] * tile(mix, step, g)
    wait_all(sin, 13)

    @pl.loop(0, 4)
    def _(i):
        entering = sin[eight(i), :]
        for g in range(GROUPS):
            rows = [rows_of(i, u, g) for u in range(4)]
            s = [
                starts(rows[u], ek_t, 1) + f_t[rows[u], :] * entering[u * 2 + g : u * 2 + g + 1, :]
                for u in range(4)
            ]
            for u in range(4):
                ek_t[rows[u], :] = s[u]
            a = [a_t[rows[u], :] for u in range(4)]
            res = [r_t[rows[u], :] for u in range(4)]
            for step in range(STEPS):
                m = tile(mix, step, g)
                s = [a[u] * s[u] + m for u in range(4)]
                conv[g, pl.ds(step * 8, 8), :] += (res[0] * s[0] + res[1] * s[1]) + (res[2] * s[2] + res[3] * s[3])

    own = at(zh, y, c)
    for g in range(GROUPS):
        for step in range(STEPS):
            turn[g, pl.ds(step, 8, stride=STEPS), :] = tile(qs, step, g) * tile(conv, step, g)
        gall[own, :, pl.ds(g * LANES, LANES)] = turn[g].astype(BF16)

    started = []

    def pass_on(block, device):
        k = len(started)
        copy = remote(gall.at[block], gall.at[block], ag_s.at[k], ag_r.at[block], device)
        copy.start()
        started.append(copy)

    def arrived(block):
        remote(gall.at[block], gall.at[block], ag_s.at[0], ag_r.at[block], tdev(1 - zh, y, c)).wait_recv()

    pass_on(own, tdev(1 - zh, y, c))
    for d in (1, 2, 3):
        pass_on(own, tdev(zh, ys[d], c))
    pass_on(own, tdev(zh, y, 1 - c))

    @pl.loop(0, 4)
    def _(i):
        tiles = [[None] * 8 for _ in range(3)]
        for g in range(GROUPS):
            for u in range(4):
                rows = rows_of(i, u, g)
                a = a_t[rows, :]
                s = ek_t[rows, :]
                res_sum = jnp.zeros((8, LANES), F32)
                dec_sum = jnp.zeros((8, LANES), F32)
                cross = jnp.zeros((8, LANES), F32)
                before = []
                for step in range(STEPS):
                    p = a * s
                    before.append(p)
                    s = p + tile(mix, step, g)
                    res_sum = res_sum + tile(gconv, step, g) * s
                    cross = a * (cross + p)
                b = starts(rows, bk_t, -1)
                bk_t[rows, :] = b
                for step in range(STEPS - 1, -1, -1):
                    b = a * b + tile(gconv, step, g)
                    dec_sum = dec_sum + before[step] * b
                scale = r_t[rows, :] * (-1.0 / SEQ)
                tiles[g][u] = collapse(res_sum)
                tiles[g][4 + u] = collapse(dec_sum * scale)
                tiles[2][u * 2 + g] = collapse(cross * scale * v_t[rows, :])
        for n in range(3):
            gtx[pl.ds(pl.multiple_of(i * GROWS + n * 8, 8), 8), :] = jnp.concatenate(tiles[n], axis=0)

    send_to_owners(gtx, grx, GROWS, 15)

    @pl.when(is_owner)
    def _():
        decay = a128_t[eight(mine), :]
        wait_all(brx, 12)

        def backward(i, b):
            otx[eight(CTX - 1 - i), :] = b
            return decay * b + brx[eight(CTX - 1 - i), :]

        lax.fori_loop(0, CTX, backward, jnp.zeros((8, LANES), F32))
        from_owner(lambda j: otx.at[eight(j)], bin_.at[eight(mine)], 14)

    def project(block):
        return dot(gall[block], weight(block))

    def gather(half):
        zt = zh if half == 0 else 1 - zh
        for d in (1, 2, 3):
            block = at(zt, ys[d], c)
            arrived(block)
            pass_on(block, tdev(zh, y, 1 - c))
            out_ref[...] += project(block)
        for d in range(4):
            block = at(zt, ys[d], 1 - c)
            arrived(block)
            out_ref[...] += project(block)

    out_ref[...] = project(own)
    gather(0)
    block = at(1 - zh, y, c)
    arrived(block)
    for d in (1, 2, 3):
        pass_on(block, tdev(zh, ys[d], c))
    pass_on(block, tdev(zh, y, 1 - c))
    out_ref[...] += project(block)

    @pl.when(is_owner)
    def _():
        wait_all(grx, 15)

        def add(j, sums):
            at_ = lambda n: grx[pl.ds(pl.multiple_of(j * GROWS + n * 8, 8), 8), :]
            return sums[0] + at_(0), sums[1] + at_(1), sums[2] + at_(2) * otx[eight(j), :]

        zero = jnp.zeros((8, LANES), F32)
        total = lax.fori_loop(0, CTX, add, (zero, zero, zero))
        for g in range(GROUPS):
            joined = [zero[0:4]] + [total[2][u * 2 + g : u * 2 + g + 1] for u in range(4)]
            gsum[pl.ds(g * 8, 8), :] = total[g] + jnp.concatenate(joined, axis=0)
        from_owner(lambda j: gsum.at[eight(j // 32)], frx.at[eight(mine)], 16)

    @pl.when(me == owner_of(0))
    def _():
        wait_all(krx, 17)
        ksum[...] = lax.fori_loop(0, CTX, lambda j, s: s + krx[j], jnp.zeros((2, LANES), F32))
        from_owner(lambda j: ksum, kfin, 18)

    for g in range(GROUPS):
        for step in range(STEPS):
            back[g, pl.ds(step * 8, 8), :] = skip_t[pl.ds(g * 8, 8), :] * tile(gconv, step, g)
    wait_all(bin_, 14)

    @pl.loop(0, 4)
    def _(i):
        entering = bin_[eight(i), :]
        for g in range(GROUPS):
            rows = [rows_of(i, u, g) for u in range(4)]
            b = [bk_t[rows[u], :] + v_t[rows[u], :] * entering[u * 2 + g : u * 2 + g + 1, :] for u in range(4)]
            a = [a_t[rows[u], :] for u in range(4)]
            res = [r_t[rows[u], :] for u in range(4)]
            for step in range(STEPS - 1, -1, -1):
                gc = tile(gconv, step, g)
                b = [a[u] * b[u] + gc for u in range(4)]
                back[g, pl.ds(step * 8, 8), :] += (res[0] * b[0] + res[1] * b[1]) + (res[2] * b[2] + res[3] * b[3])

    for j, (left, right) in enumerate(((grad, conv), (back, vs), (back, ks))):
        for g in range(GROUPS):
            for step in range(STEPS):
                turn[g, pl.ds(step, 8, stride=STEPS), :] = tile(left, step, g) * tile(right, step, g)
            proj_ref[j, pl.ds(g * LANES, LANES), :] = turn[g].T

    gather(1)

    wait_all(frx, 16)
    wait_all(kfin, 18)
    chosen = lax.broadcasted_iota(jnp.int32, (8, LANES), 1) == lax.rem(me, 32) * 4 + lax.broadcasted_iota(
        jnp.int32, (8, LANES), 0
    )
    chosen = jnp.where(chosen, 1.0, 0.0).astype(F32)

    def pick(x):
        return lax.dot_general(
            chosen, x, (((1,), (1,)), ((), ())), precision=HIGHEST, preferred_element_type=F32
        )[0:4]

    res_ref[...] = pick(jnp.concatenate([frx[pl.ds(o * 8, 4), :] for o in range(OWNERS)], axis=0))
    dec_ref[...] = pick(jnp.concatenate([frx[pl.ds(o * 8 + 4, 4), :] for o in range(OWNERS)], axis=0))
    my_skip = jnp.where(me // 32 == 0, kfin[0:1, :], kfin[1:2, :])
    skip_ref[...] = lax.dot_general(
        my_skip, chosen, (((1,), (1,)), ((), ())), precision=HIGHEST, preferred_element_type=F32
    )[:, 0:4]

    for h in range(2):
        core[h].wait_send()
        for copy in sums[h]:
            copy.wait_send()
    zcopy.wait_send()
    for copy in started:
        copy.wait_send()
    sent_to_owners(etx, OROWS, 11)
    sent_to_owners(btx, OROWS, 12)
    sent_to_owners(gtx, GROWS, 15)

    @pl.when(is_owner)
    def _():
        for k in (13, 14, 16):
            wait_sent(stx.at[pl.ds(0, (CTX - 1) * OROWS)], k)

    @pl.when(me == owner_of(0))
    def _():
        wait_sent(krx.at[pl.ds(0, CTX - 1)], 18)

    @pl.when(me != owner_of(0))
    def _():
        wait_sent(ktx, 17)


def local(streams, out_weight, cotangent, residues, decay_rates, skip_gain):
    channels, width = streams.shape[0], out_weight.shape[1]
    vmem = pl.BlockSpec(memory_space=pltpu.VMEM)
    f, h = lambda *s: pltpu.VMEM(s, F32), lambda *s: pltpu.VMEM(s, BF16)
    block_out, proj, residue_grad, decay_grad, skip_grad = pl.pallas_call(
        kernel,
        name="hyena",
        out_shape=(
            jax.ShapeDtypeStruct((CHUNK, width), F32),
            jax.ShapeDtypeStruct((3, channels, CHUNK), F32),
            jax.ShapeDtypeStruct((4, 16), F32),
            jax.ShapeDtypeStruct((4, 16), F32),
            jax.ShapeDtypeStruct((1, 4), F32),
        ),
        in_specs=[pl.BlockSpec(memory_space=pl.ANY)] * 6,
        out_specs=(vmem,) * 5,
        scratch_shapes=[
            f(4, 16), f(4, 16), f(1, 4), h(3, 256, 128), h(128, 512), h(4096, 512),
            f(2, 128), f(CTX, 2, 128), f(128, 128), f(2, 512, 256), f(2, 512, 256), f(2, 512, 256),
            f(2, 3, 128, 256), f(2, 3, 128, 256), f(128, 256), f(128, 256),
            f(32, 128), f(512, 128), f(512, 128), f(32, 128),
            f(32, 128), f(512, 128), f(512, 128), f(32, 128),
            f(96, 128), f(CTX * GROWS, 128), f(16, 128), f(32, 128),
            f(2, 128), f(CTX, 2, 128), f(2, 128), f(2, 128),
            f(256, 128), f(256, 128), f(256, 128), f(256, 128), f(256, 128), f(256, 128), f(256, 128),
            f(32, 128), f(16, 128),
            f(2, 128, 128), f(2, 128, 128), f(2, 128, 128), f(2, 128, 128), f(2, 128, 128),
            f(2, 128, 128), f(2, 128, 128), f(2, 128, 128), f(2, 128, 128), h(16, 128, 256),
            pltpu.SemaphoreType.DMA((19,)), pltpu.SemaphoreType.DMA((19,)),
            pltpu.SemaphoreType.DMA((15,)), pltpu.SemaphoreType.DMA((16,)), pltpu.SemaphoreType.DMA((6,)),
        ],
        compiler_params=pltpu.CompilerParams(
            collective_id=0, has_side_effects=True, vmem_limit_bytes=60 * 2**20
        ),
    )(residues, decay_rates, skip_gain.reshape(1, 4), streams.transpose(1, 0, 2), cotangent, out_weight)
    return block_out, proj.transpose(1, 0, 2), residue_grad, decay_grad, skip_grad.reshape(4)


def solution(mesh):
    return jax.shard_map(
        local,
        mesh=mesh,
        in_specs=(
            P("tensor", None, "context"),
            P(None, "tensor"),
            P("context", "tensor"),
            P(("tensor", "context"), None),
            P(("tensor", "context"), None),
            P(("tensor", "context")),
        ),
        out_specs=(
            P("context", "tensor"),
            P("tensor", None, "context"),
            P(("tensor", "context"), None),
            P(("tensor", "context"), None),
            P(("tensor", "context")),
        ),
        check_vma=False,
    )
```

time: 691 us -> 121 us (0.18)
  waiting for transfers between devices: 543 us -> 0 us
  Pallas kernels: 0 us -> 111 us
  starting transfers between devices: 58.2 us -> 0 us
  matrix products: 33.8 us -> 0 us
  blocking collectives: 29.5 us -> 0 us
  between operations: 14.3 us -> 0.64 us
  other arithmetic: 7.86 us -> 0 us
    psum x1 -> x0, waiting for transfers between devices: 419 us -> none  [local(): lax.psum(lax.dot_general(weight_rows, cotangent, (((1,), (1,)), ((), ()))...]
    pallas_call x0 -> x1, Pallas kernels: none -> 111 us  [local(): pl.pallas_call(kernel, name='hyena', out_shape=(jax.ShapeDtypeStruct((CHU...]
    all_gather x1 -> x0, waiting for transfers between devices: 91 us -> none  [local(): lax.all_gather(gated, 'tensor', axis=0, tiled=True)]
    all_to_all x3 -> x0, starting transfers between devices: 57.9 us -> none  [the longest x1 29.8 us: local(): lax.all_to_all(product_rows, 'context', split_axis=0, concat_axis=1, tile...]
    dot_general x17 -> x0, matrix products: 33.8 us -> none  [the longest x1 4.77 us: local(): lax.dot_general(weight_rows, cotangent, (((1,), (1,)), ((), ())), preferr...]
    all_to_all x3 -> x0, waiting for transfers between devices: 33.4 us -> none  [the longest x1 19.3 us: local(): lax.all_to_all(grad_conv, 'context', split_axis=0, concat_axis=1, tiled=T...]
    all_to_all x1 -> x0, blocking collectives: 29.5 us -> none  [local(): lax.all_to_all(conv_rows, 'context', split_axis=1, concat_axis=0, tiled=T...]
  transfers between devices with their start and end apart: 5 -> 0, of which waited for: 4 -> 0; matrix products, arithmetic and copies ran while one was open for 2% -> 0% of each run, Pallas kernels for 0% -> 0%
where the time goes in v1:
time: 121 us; the launch traced here: 119 us
  Pallas kernels  111 us (92%)
  local copies, waits for them, and re-layouts  7.04 us (6%)
    pallas_call x1, Pallas kernels, local(): pl.pallas_call(kernel, name='hyena', out_shape=(jax.ShapeDtypeStruct((CHU...  111 us
    unnamed x5, local copies, waits for them, and re-layouts  7.04 us

profile of v1, /device:TPU:1, one launch (start us, length us, event | category | flops | bytes accessed | tf_op | source)
XLA Modules:
  0.0 119.1 jit_solution(276524172872377016)
XLA Ops:
  0.6 111.4 %hyena.1 = (f32[128,512]{1,0:T(8,128)}, f32[3,256,128]{2,1,0:T(8,128)}, f32[4,16]{1,0:T(4,128)}, f32[4,16]{1,0:T(4,128)}, f32[1,4]{1,0:T(1,128)}) custom-call(f32[4,16]{1,0:T(4,128)} %res_hbm.1, f32[4,16]{1,0:T(4,128)} %dec_hbm.1, f32[1,4]{1,0:T(1,128)} %bitcast.6, bf16[3,256,128]{2,1,0:T(8,128)(2,1)} %bitcast.5, bf16[128,512]{1,0:T(8,128)(2,1)} %cot_hbm.1, ...), custom_call_target="tpu_custom_call" | custom-call | tf_op jit(solution)/shard_map/hyena/pallas_call | solution.py:522
  112.0 1.7 %copy.16 = f32[128,512]{1,0:T(8,128)} copy(f32[128,512]{1,0:T(8,128)} %get-tuple-element.20) | data formatting | bytes 524288
  113.7 1.8 %copy.17 = f32[256,3,128]{2,0,1:T(8,128)} copy(f32[256,3,128]{2,0,1:T(8,128)} %bitcast.4) | data formatting | bytes 786432
  115.5 1.2 %copy.18 = f32[4,16]{1,0:T(4,128)} copy(f32[4,16]{1,0:T(4,128)} %get-tuple-element.22) | data formatting | bytes 512
  116.7 1.2 %copy.19 = f32[4,16]{1,0:T(4,128)} copy(f32[4,16]{1,0:T(4,128)} %get-tuple-element.23) | data formatting | bytes 512
  118.0 1.1 copy.20
